TPU v7x, 1024 devices: a whole 4x8x16 slice. The times are simulated.
1024 devices in a mesh: expert: 32 (over y, z_lo), dp: 32 (over z_hi, x, core).
Axes of the slice: x: 4, y: 8, z: 16 (z_hi: 4, z_lo: 4; z = z_hi * 4 + z_lo), core: 2. Of those that a mesh axis runs over, the one named last changes fastest.
Arguments:
- tokens: bfloat16 [131072, 2048], P(('expert', 'dp')), may hold values from -24 to 24
- routes: int32 [131072, 1], P(('expert', 'dp')), may hold values from 0 to 31; in each aligned block of 128 rows (0 to 127, 128 to 255, ...) at most 6 rows name the same one
- route_weight: float32 [131072, 1], P(('expert', 'dp')), may hold values from 0.25 to 1
- w_in: bfloat16 [32, 2048, 768], P('expert'), may hold values from -0.125 to 0.125
- w_out: bfloat16 [32, 2048, 384], P('expert'), may hold values from -0.3125 to 0.3125
- out_grad: bfloat16 [131072, 2048], P(('expert', 'dp')), may hold values from -6 to 6
Outputs:
- mixed: bfloat16 [131072, 2048], P(('expert', 'dp'))
- token_grad: bfloat16 [131072, 2048], P(('expert', 'dp'))
- grad_in: bfloat16 [32, 2048, 768], P('expert', 'dp')
- grad_out: bfloat16 [32, 2048, 384], P('expert', 'dp')
Inputs may be any that keep to these rules, and one draw needn't show every extreme that they name: `routes`: in the 128 rows of one device no expert is named more than 6 times, and in every draw some device names some expert exactly 6 times.
All inputs are finite; a program needn't handle non-finite values.
Results may differ from a plain program's by a relative error of at most 0.02.
Values may be sent and summed in bfloat16 or wider, within the bound.
A program may use at most 64 MiB of HBM per device.

v0:
```python
import jax
import jax.numpy as jnp
from jax import lax
from jax.sharding import PartitionSpec as P


def placement_rows(routes, experts, capacity):
    chosen = routes[:, 0]
    onehot = (chosen[:, None] == jnp.arange(experts, dtype=jnp.int32)[None, :]).astype(jnp.int32)
    ranks = jnp.sum(jnp.cumsum(onehot, axis=0) * onehot, axis=1) - 1
    target = chosen * capacity + ranks
    slots = jnp.arange(experts * capacity, dtype=jnp.int32)
    return (slots[:, None] == target[None, :]).astype(jnp.bfloat16)


def contract_rows(left, right):
    return lax.dot_general(
        left, right, (((0,), (0,)), ((), ())), preferred_element_type=jnp.float32
    )


def contract_cols(left, right):
    return lax.dot_general(
        left, right, (((1,), (1,)), ((), ())), preferred_element_type=jnp.float32
    )


def per_device(tokens, routes, route_weight, w_in, w_out, out_grad):
    token_count = tokens.shape[0]
    experts = w_in.shape[0] * lax.axis_size("expert")
    capacity = 3 * token_count // (2 * experts)
    width = w_out.shape[2]
    replicas = lax.axis_size("dp")
    first = w_in[0]
    second = w_out[0]
    placer = placement_rows(routes, experts, capacity)
    send_rows = jnp.dot(placer, tokens, preferred_element_type=jnp.float32).astype(jnp.bfloat16)
    cotangent = (route_weight * out_grad.astype(jnp.float32)).astype(jnp.bfloat16)
    send_cot = jnp.dot(placer, cotangent, preferred_element_type=jnp.float32).astype(jnp.bfloat16)
    rows_in, rows_cot = (
        lax.all_to_all(send_rows, "expert", split_axis=0, concat_axis=0, tiled=True),
        lax.all_to_all(send_cot, "expert", split_axis=0, concat_axis=0, tiled=True),
    )
    gate_up = jnp.dot(rows_in, first, preferred_element_type=jnp.float32)
    gate = gate_up[:, :width]
    upper = gate_up[:, width:]
    sigmoid_gate = jax.nn.sigmoid(gate)
    activated = gate * sigmoid_gate
    hidden = (activated * upper).astype(jnp.bfloat16)
    outputs = contract_cols(hidden, second).astype(jnp.bfloat16)
    gate, upper, sigmoid_gate, activated, hidden, outputs = (
        gate,
        upper,
        sigmoid_gate,
        activated,
        hidden,
        outputs,
    )
    grad_hidden = jnp.dot(rows_cot, second, preferred_element_type=jnp.float32)
    grad_gate = grad_hidden * upper * sigmoid_gate * (1.0 + gate * (1.0 - sigmoid_gate))
    grad_upper = grad_hidden * activated
    grad_both = jnp.concatenate([grad_gate, grad_upper], axis=1).astype(jnp.bfloat16)
    grad_rows = contract_cols(grad_both, first).astype(jnp.bfloat16)
    back_out, back_grad = (
        lax.all_to_all(outputs, "expert", split_axis=0, concat_axis=0, tiled=True),
        lax.all_to_all(grad_rows, "expert", split_axis=0, concat_axis=0, tiled=True),
    )
    token_out = contract_rows(placer, back_out)
    mixed = (route_weight * token_out).astype(jnp.bfloat16)
    token_grad = contract_rows(placer, back_grad).astype(jnp.bfloat16)
    term_first = contract_rows(rows_in, grad_both)
    term_second = contract_rows(rows_cot, hidden)
    sum_first, sum_second = (
        lax.psum_scatter(
            term_first.astype(jnp.bfloat16), "dp", scatter_dimension=0, tiled=True
        ).astype(jnp.float32),
        lax.psum_scatter(
            term_second.astype(jnp.bfloat16), "dp", scatter_dimension=0, tiled=True
        ).astype(jnp.float32),
    )
    grad_in = (sum_first / replicas).astype(jnp.bfloat16)[None]
    grad_out = (sum_second / replicas).astype(jnp.bfloat16)[None]
    return (mixed, token_grad, grad_in, grad_out)


def solution(mesh):
    in_specs = (
        P(("expert", "dp"), None),
        P(("expert", "dp"), None),
        P(("expert", "dp"), None),
        P("expert", None, None),
        P("expert", None, None),
        P(("expert", "dp"), None),
    )
    out_specs = (
        P(("expert", "dp"), None),
        P(("expert", "dp"), None),
        P("expert", "dp", None),
        P("expert", "dp", None),
    )
    return jax.shard_map(
        per_device, mesh=mesh, in_specs=in_specs, out_specs=out_specs, check_vma=False
    )
```

profile of v0, /device:TPU:16, one launch (start us, length us, event | category | flops | bytes accessed | tf_op | source)
XLA Modules:
  0.0 374.6 jit_solution(17621303763480446354)
XLA Ops:
  7.2 0.0 copy-start
  7.2 0.9 fusion.14
  8.1 0.2 reduce_window_sum.11
  8.2 0.8 select_reduce_fusion
  9.1 0.7 add_add_fusion
  9.7 2.3 convolution_convert_fusion.3
  12.0 0.0 copy-start.3
  12.0 2.2 all_to_all.32
  14.2 17.3 %all-to-all-start = ((bf16[32,6,2048]{2,1,0:T(8,128)(2,1)}), bf16[32,6,2048]{2,1,0:T(8,128)(2,1)}, u32[]{:S(2)}, u32[]{:S(2)}) async-start(bf16[32,6,2048]{2,1,0:T(8,128)(2,1)} %all_to_all.32), calls=%async_computation | async-start | bytes 2097152 | tf_op jit(solution)/shard_map/all_to_all | solution.py:41
  31.5 0.0 copy-done.3
  31.5 2.4 convolution_convert_fusion.2
  33.9 2.2 all_to_all.38
  36.1 18.6 %all-to-all-done = bf16[32,6,2048]{2,1,0:T(8,128)(2,1)} async-done(((bf16[32,6,2048]{2,1,0:T(8,128)(2,1)}), bf16[32,6,2048]{2,1,0:T(8,128)(2,1)}, u32[]{:S(2)}, u32[]{:S(2)}) %all-to-all-start) | async-done | bytes 786464 | tf_op jit(solution)/shard_map/all_to_all | solution.py:41
  54.7 6.4 %all-to-all-start.2 = ((bf16[32,6,2048]{2,1,0:T(8,128)(2,1)}), bf16[32,6,2048]{2,1,0:T(8,128)(2,1)}, u32[]{:S(2)}, u32[]{:S(2)}) async-start(bf16[32,6,2048]{2,1,0:T(8,128)(2,1)} %all_to_all.38), calls=%async_computation.2 | async-start | bytes 2097152 | tf_op jit(solution)/shard_map/all_to_all | solution.py:42
  61.1 0.0 reduce-scatter.5.cloned.1.call-start
  61.2 2.1 all_to_all.34
  63.3 0.0 copy-done
  63.3 2.8 fusion.2
  66.1 22.0 %all-to-all-done.2 = bf16[32,6,2048]{2,1,0:T(8,128)(2,1)} async-done(((bf16[32,6,2048]{2,1,0:T(8,128)(2,1)}), bf16[32,6,2048]{2,1,0:T(8,128)(2,1)}, u32[]{:S(2)}, u32[]{:S(2)}) %all-to-all-start.2) | async-done | bytes 786464 | tf_op jit(solution)/shard_map/all_to_all | solution.py:42
  88.0 2.1 all_to_all.40
  90.2 0.0 copy-start.1
  90.2 3.1 multiply_convert_fusion.3
  93.3 0.0 copy-done.1
  93.3 1.9 convolution_convert_fusion.1
  95.2 0.0 reduce-scatter.5.cloned.1.call-update
  95.2 3.0 fusion.4
  98.2 2.2 all_to_all.41
  100.4 5.9 %all-to-all-start.3 = ((bf16[32,6,2048]{2,1,0:T(8,128)(2,1)}), bf16[32,6,2048]{2,1,0:T(8,128)(2,1)}, u32[]{:S(2)}, u32[]{:S(2)}) async-start(bf16[32,6,2048]{2,1,0:T(8,128)(2,1)} %all_to_all.41), calls=%async_computation.3 | async-start | bytes 2097152 | tf_op jit(solution)/shard_map/all_to_all | solution.py:66
  106.4 0.0 reduce-scatter.3.cloned.1.call-start
  106.4 3.8 %convolution_convert_fusion = bf16[2048,768]{1,0:T(8,128)(2,1)} fusion(bf16[192,2048]{1,0:T(8,128)(2,1)} %all_to_all.34, bf16[192,384]{1,0:T(8,128)(2,1)} %get-tuple-element.5, bf16[192,384]{1,0:T(8,128)(2,1)S(1)} %get-tuple-element.4), kind=kOutput, calls=%fused_computation | convolution fusion | flops 606142464 | bytes 4227072 | tf_op jit(solution)/shard_map/dot_general | solution.py:17
  110.3 0.0 reduce-scatter.3.cloned.1.call-update
  110.3 3.1 convolution_convert_fusion.4
  113.4 2.2 all_to_all.35
  115.5 17.9 %all-to-all-done.3 = bf16[32,6,2048]{2,1,0:T(8,128)(2,1)} async-done(((bf16[32,6,2048]{2,1,0:T(8,128)(2,1)}), bf16[32,6,2048]{2,1,0:T(8,128)(2,1)}, u32[]{:S(2)}, u32[]{:S(2)}) %all-to-all-start.3) | async-done | bytes 786464 | tf_op jit(solution)/shard_map/all_to_all | solution.py:66
  133.4 6.6 %all-to-all-start.1 = ((bf16[32,6,2048]{2,1,0:T(8,128)(2,1)}), bf16[32,6,2048]{2,1,0:T(8,128)(2,1)}, u32[]{:S(2)}, u32[]{:S(2)}) async-start(bf16[32,6,2048]{2,1,0:T(8,128)(2,1)} %all_to_all.35), calls=%async_computation.1 | async-start | bytes 2097152 | tf_op jit(solution)/shard_map/all_to_all | solution.py:65
  140.0 86.6 %reduce-scatter.5.cloned.1.call-done = bf16[64,384]{1,0:T(8,128)(2,1)} async-done(((bf16[2048,384]{1,0:T(8,128)(2,1)}), bf16[64,384]{1,0:T(8,128)(2,1)}) %reduce-scatter.5.cloned.1.call-update) | async-done | bytes 49168 | tf_op jit(solution)/shard_map/reduce_scatter | solution.py:77
  226.6 1.4 fusion.15
  228.0 2.1 all_to_all.43
  230.2 0.0 all-to-all-done.1
  230.2 2.2 all_to_all.37
  232.3 0.0 copy-start.2
  232.3 2.4 convolution_convert_fusion.5
  234.7 0.0 copy-done.2
  234.7 1.2 fusion.7
  235.8 130.4 %reduce-scatter.3.cloned.1.call-done = bf16[64,768]{1,0:T(8,128)(2,1)} async-done(((bf16[2048,768]{1,0:T(8,128)(2,1)}), bf16[64,768]{1,0:T(8,128)(2,1)}) %reduce-scatter.3.cloned.1.call-update) | async-done | bytes 98320 | tf_op jit(solution)/shard_map/reduce_scatter | solution.py:74
  366.2 1.6 fusion.13
Async XLA Ops:
  7.2 56.1 %copy-start = (bf16[1,2048,768]{2,1,0:T(8,128)(2,1)S(1)}, bf16[1,2048,768]{2,1,0:T(8,128)(2,1)}, u32[]{:S(2)}) copy-start(bf16[1,2048,768]{2,1,0:T(8,128)(2,1)} %param.9) | copy-start | bytes 9437188
  12.0 19.5 %copy-start.3 = (f32[128,1]{0,1:T(1,128)S(1)}, f32[128,1]{0,1:T(1,128)}, u32[]{:S(2)}) copy-start(f32[128,1]{0,1:T(1,128)} %param.8) | copy-start | bytes 1540
  14.2 40.5 %all-to-all-start = ((bf16[32,6,2048]{2,1,0:T(8,128)(2,1)}), bf16[32,6,2048]{2,1,0:T(8,128)(2,1)}, u32[]{:S(2)}, u32[]{:S(2)}) async-start(bf16[32,6,2048]{2,1,0:T(8,128)(2,1)} %all_to_all.32), calls=%async_computation | async-start | bytes 2097152 | tf_op jit(solution)/shard_map/all_to_all | solution.py:41
  54.7 33.3 %all-to-all-start.2 = ((bf16[32,6,2048]{2,1,0:T(8,128)(2,1)}), bf16[32,6,2048]{2,1,0:T(8,128)(2,1)}, u32[]{:S(2)}, u32[]{:S(2)}) async-start(bf16[32,6,2048]{2,1,0:T(8,128)(2,1)} %all_to_all.38), calls=%async_computation.2 | async-start | bytes 2097152 | tf_op jit(solution)/shard_map/all_to_all | solution.py:42
  61.1 165.5 %reduce-scatter.5.cloned.1.call-start = ((), (), s32[]{:S(2)}) async-start(), calls=%async_computation.7 | async-start | bytes 1622016 | tf_op jit(solution)/shard_map/reduce_scatter | solution.py:77
  90.2 3.1 copy-start.1
  100.4 33.0 %all-to-all-start.3 = ((bf16[32,6,2048]{2,1,0:T(8,128)(2,1)}), bf16[32,6,2048]{2,1,0:T(8,128)(2,1)}, u32[]{:S(2)}, u32[]{:S(2)}) async-start(bf16[32,6,2048]{2,1,0:T(8,128)(2,1)} %all_to_all.41), calls=%async_computation.3 | async-start | bytes 2097152 | tf_op jit(solution)/shard_map/all_to_all | solution.py:66
  106.4 259.8 %reduce-scatter.3.cloned.1.call-start = ((), (), s32[]{:S(2)}) async-start(), calls=%async_computation.6 | async-start | bytes 3244032 | tf_op jit(solution)/shard_map/reduce_scatter | solution.py:74
  133.4 96.7 %all-to-all-start.1 = ((bf16[32,6,2048]{2,1,0:T(8,128)(2,1)}), bf16[32,6,2048]{2,1,0:T(8,128)(2,1)}, u32[]{:S(2)}, u32[]{:S(2)}) async-start(bf16[32,6,2048]{2,1,0:T(8,128)(2,1)} %all_to_all.35), calls=%async_computation.1 | async-start | bytes 2097152 | tf_op jit(solution)/shard_map/all_to_all | solution.py:65
  232.3 2.4 copy-start.2
Sparse Core Ops, SparseCore 0:
  95.4 131.1 reduce-scatter.4
  232.2 133.9 reduce-scatter.2
where the time goes:
time: 376 us; the launch traced here: 375 us
  waiting for transfers between devices  275 us (73%)
  starting transfers between devices  36.2 us (10%)
  matrix products  25.8 us (7%)
  local copies, waits for them, and re-layouts  17.4 us (5%)
  between operations  14.1 us (4%)
  other arithmetic  5.53 us (1%)
    reduce_scatter x1, waiting for transfers between devices, per_device(): lax.psum_scatter(term_first.astype(jnp.bfloat16), 'dp', scatter_dimension...  130 us
    reduce_scatter x1, waiting for transfers between devices, per_device(): lax.psum_scatter(term_second.astype(jnp.bfloat16), 'dp', scatter_dimensio...  86.6 us
    all_to_all x1, waiting for transfers between devices, per_device(): lax.all_to_all(send_cot, 'expert', split_axis=0, concat_axis=0, tiled=True)  22 us
    all_to_all x1, waiting for transfers between devices, per_device(): lax.all_to_all(send_rows, 'expert', split_axis=0, concat_axis=0, tiled=True)  18.6 us
    all_to_all x1, waiting for transfers between devices, per_device(): lax.all_to_all(grad_rows, 'expert', split_axis=0, concat_axis=0, tiled=True)  17.9 us
    all_to_all x1, starting transfers between devices, per_device(): lax.all_to_all(send_rows, 'expert', split_axis=0, concat_axis=0, tiled=True)  17.3 us
    dot_general x4, matrix products, contract_rows(): lax.dot_general(left, right, (((0,), (0,)), ((), ())), preferred_element_...  9.24 us
  transfers between devices with their start and end apart: 6, of which 5 were waited for; matrix products, arithmetic and copies ran while one was open for 5% of the time, Pallas kernels for 0%

commit v1 on v0

v1 whole, which is shorter than its diff:
```python
import functools

import jax
import jax.numpy as jnp
from jax import lax
from jax.experimental import pallas as pl
from jax.experimental.pallas import tpu as pltpu
from jax.sharding import PartitionSpec as P

MESH = pl.DeviceIdType.MESH
BF = jnp.bfloat16
F32 = jnp.float32

D = 2048
F1 = 768
F2 = 384
FF = F1 + F2
ROWS = 192
TOK = 128
LANES = 128
TILE = 16
FHALF = FF // 2
FQ = FHALF // 2
FD = FQ // 2
NT = (((1,), (1,)), ((), ()))
WINDOW = (-1, 0, 1, 2)


def slot_tables(routes):
    chosen = routes[:, 0]
    at = jnp.arange(TOK, dtype=jnp.int32)
    earlier = (chosen[:, None] == chosen[None, :]) & (at[None, :] < at[:, None])
    rank = jnp.sum(earlier.astype(jnp.int32), axis=1)
    group = (rank // 3) * 32 + chosen
    inner = rank % 3
    place = group * 3 + inner
    slots = jnp.arange(ROWS, dtype=jnp.int32)
    source = TOK + jnp.sum(
        jnp.where(place[None, :] == slots[:, None], at[None, :] - TOK, 0), axis=1
    )
    return source, group, inner


def kernel(
    source, group, inner, tokens, out_grad, weight, w1_any, w2_any,
    mixed, token_grad, grad_in, grad_out,
    w1, w2, perm, tiles_t, tiles_c, stage, mid, landed, mat_x, mat_c, gates, qh, qht, mat_y,
    ytile, zback, back_y, back_r, part, other, summed,
    xrelay, xacc, from_l, from_r, zsum, zrelay, zacc, zfrom_l, zfrom_r, final,
    w_sem, ys, yr, yl, zs, zr, zl_sem, rzs, rzr, rzl, rys, ryr, ryl,
    cs, cr, xs, xr, gs, gr, fs, fr,
):
    e = lax.axis_index("expert")
    d = lax.axis_index("dp")
    y, zl = e // 4, e % 4
    zh, x, c = d // 8, (d // 2) % 4, d % 2
    z = zh * 4 + zl
    sign = 1 - 2 * c

    def device(y_at, z_at, x_at, c_at):
        return {"expert": y_at * 4 + z_at % 4, "dp": (z_at // 4) * 8 + x_at * 2 + c_at}

    def y_dev(step):
        return device((y + step) % 8, z, x, c)

    def z_dev(step):
        return device(y, (z + step + 16) % 16, x, c)

    def x_dev(step):
        return device(y, z, (x + step + 4) % 4, c)

    twin = device(y, z, x, 1 - c)

    def remote(src, dst, send, recv, to):
        return pltpu.make_async_remote_copy(
            src_ref=src, dst_ref=dst, send_sem=send, recv_sem=recv, device_id=to, device_id_type=MESH
        )

    barrier = pltpu.get_barrier_semaphore()

    def greet(to):
        pl.semaphore_signal(barrier, inc=1, device_id=to, device_id_type=MESH)

    for step in range(1, 8):
        greet(y_dev(step))
    for step in (-4, -2, -1, 1, 2, 4):
        greet(z_dev(step))
    for step in (-1, 1):
        greet(x_dev(step))
    greet(twin)

    w_copies = (
        pltpu.make_async_copy(w1_any.at[0], w1, w_sem.at[0]),
        pltpu.make_async_copy(w2_any.at[0], w2, w_sem.at[1]),
    )
    for copy in w_copies:
        copy.start()

    row_at = lax.broadcasted_iota(jnp.int32, (256, 256), 0)
    col_at = lax.broadcasted_iota(jnp.int32, (256, 256), 1)
    perm[...] = jnp.where(col_at == (row_at % 16) * 16 + row_at // 16, 1.0, 0.0).astype(BF)

    def to_tiles(rows32):
        cols = [
            jnp.concatenate(
                [rows32[:16, k * LANES : (k + 1) * LANES], rows32[16:, k * LANES : (k + 1) * LANES]], axis=1
            )
            for k in range(16)
        ]
        out = jnp.dot(perm[...], jnp.concatenate(cols, axis=0), preferred_element_type=F32).astype(BF)
        return out[:, :LANES].reshape(16, TILE, LANES), out[:, LANES:].reshape(16, TILE, LANES)

    def from_tiles(first, second):
        both = jnp.concatenate([first.reshape(256, LANES), second.reshape(256, LANES)], axis=1)
        return jnp.dot(perm[...], both, preferred_element_type=F32)

    tiles_t[TOK] = jnp.zeros((TILE, LANES), BF)
    tiles_c[TOK] = jnp.zeros((TILE, LANES), BF)

    def y_copy(a, h, step):
        there = (y + step) % 8
        return remote(
            stage.at[a, h, pl.ds(there * 4, 4)],
            mid.at[a, h, :, pl.ds(y * 3, 3)],
            ys.at[a, h, step - 1],
            yr.at[a, h, step - 1],
            y_dev(step),
        )

    def y_self(a, h):
        return pltpu.make_async_copy(
            stage.at[a, h, pl.ds(y * 4, 4)], mid.at[a, h, :, pl.ds(y * 3, 3)], yl.at[a, h]
        )

    def step_of(n):
        half = n // 2 + 1
        return half + (n % 2) * (8 - 2 * half)

    def over_steps(body):
        def once(n, carry):
            body(step_of(n))
            return carry

        lax.fori_loop(0, 7, once, 0)

    def split_tokens(i, carry):
        lo, hi = to_tiles(tokens[pl.ds(i * 32, 32), :])
        tiles_t[pl.ds(i * 32, 16)] = lo
        tiles_t[pl.ds(i * 32 + 16, 16)] = hi
        return carry

    lax.fori_loop(0, 4, split_tokens, 0)

    def gather(a, h, tiles):
        def once(i, carry):
            for s in range(3):
                stage[a, h, i, s] = tiles[source[(h * 32 + i) * 3 + s]]
            return carry

        lax.fori_loop(0, 32, once, 0, unroll=4)

    gather(0, 0, tiles_t)
    pl.semaphore_wait(barrier, 16)
    over_steps(lambda step: y_copy(0, 0, step).start())
    y_self(0, 0).start()
    gather(0, 1, tiles_t)
    over_steps(lambda step: y_copy(0, 1, step).start())
    y_self(0, 1).start()

    def split_cot(i, carry):
        rows = pl.ds(i * 32, 32)
        cot = (weight[rows, :] * out_grad[rows, :].astype(F32)).astype(BF)
        lo, hi = to_tiles(cot)
        tiles_c[pl.ds(i * 32, 16)] = lo
        tiles_c[pl.ds(i * 32 + 16, 16)] = hi
        return carry

    lax.fori_loop(0, 4, split_cot, 0)
    for h in range(2):
        gather(1, h, tiles_c)
        over_steps(lambda step: y_copy(1, h, step).start())
        y_self(1, h).start()

    def z_copy(a, h, k):
        to = (z + sign * WINDOW[k] + 16) % 16
        return remote(
            mid.at[a, h, to % 4], landed.at[a, h, pl.ds(k * 24, 24)], zs.at[a, h, k], zr.at[a, h, k],
            device(y, to, x, c),
        )

    def z_self(a, h):
        return pltpu.make_async_copy(mid.at[a, h, zl], landed.at[a, h, pl.ds(24, 24)], zl_sem.at[a, h])

    def pass_on(a, h):
        over_steps(lambda step: y_copy(a, h, step).wait_recv())
        y_self(a, h).wait()
        for k in (3, 0, 2):
            z_copy(a, h, k).start()
        z_self(a, h).start()

    def take(a, h, mat):
        for k in (0, 2, 3):
            z_copy(a, h, k).wait_recv()
        z_self(a, h).wait()

        def once(i, carry):
            out = from_tiles(landed[a, h, pl.ds(i * 32, 16)], landed[a, h, pl.ds(i * 32 + 16, 16)])
            lo = pl.multiple_of(h * 96 + i * 32, 32)
            for k in range(16):
                cols = slice(k * LANES, (k + 1) * LANES)
                mat[pl.ds(lo, 16), cols] = out[k * 16 : (k + 1) * 16, :LANES].astype(BF)
                mat[pl.ds(lo + 16, 16), cols] = out[k * 16 : (k + 1) * 16, LANES:].astype(BF)
            return carry

        lax.fori_loop(0, 3, once, 0)

    def rz_copy(a, h, k):
        to = (z - sign * WINDOW[k] + 16) % 16
        return remote(
            ytile.at[a, h, pl.ds(k * 24, 24)], zback.at[a, h, zl], rzs.at[a, h, k], rzr.at[a, h, k],
            device(y, to, x, c),
        )

    def rz_self(a, h):
        return pltpu.make_async_copy(ytile.at[a, h, pl.ds(24, 24)], zback.at[a, h, zl], rzl.at[a, h])

    backs = (back_y, back_r)

    def ry_copy(a, h, step):
        there = (y + step) % 8
        return remote(
            zback.at[a, h, :, pl.ds(there * 3, 3)],
            backs[a].at[pl.ds(h * 32 + y * 4, 4)],
            rys.at[a, h, step - 1],
            ryr.at[a, h, step - 1],
            y_dev(step),
        )

    def ry_self(a, h):
        return pltpu.make_async_copy(
            zback.at[a, h, :, pl.ds(y * 3, 3)], backs[a].at[pl.ds(h * 32 + y * 4, 4)], ryl.at[a, h]
        )

    def send_back(a):
        for h in range(2):
            def once(i, carry):
                lo, hi = to_tiles(mat_y[pl.ds(pl.multiple_of(h * 96 + i * 32, 32), 32), :])
                ytile[a, h, pl.ds(i * 32, 16)] = lo
                ytile[a, h, pl.ds(i * 32 + 16, 16)] = hi
                return carry

            lax.fori_loop(0, 3, once, 0)
            for k in (3, 0, 2):
                rz_copy(a, h, k).start()
            rz_self(a, h).start()

    def pass_back(a, h):
        for k in (0, 2, 3):
            rz_copy(a, h, k).wait_recv()
        rz_self(a, h).wait()
        over_steps(lambda step: ry_copy(a, h, step).start())
        ry_self(a, h).start()

    def contract_back(left, width, weights):
        def once(n, carry):
            at = pl.multiple_of(n * 256, 256)
            out = lax.dot_general(left, weights[pl.ds(at, 256), :], NT, preferred_element_type=F32)
            mat_y[:, pl.ds(at, 256)] = out.astype(BF)
            return carry

        lax.fori_loop(0, D // 256, once, 0)

    for copy in w_copies:
        copy.wait()
    pass_on(0, 0)
    pass_on(0, 1)
    take(0, 0, mat_x)
    take(0, 1, mat_x)

    def gates_once(n, carry):
        at = pl.multiple_of(n * 256, 256)
        gates[:, pl.ds(at, 256)] = jnp.dot(mat_x[...], w1[:, pl.ds(at, 256)], preferred_element_type=F32)
        return carry

    lax.fori_loop(0, F1 // 256, gates_once, 0)

    def hidden_once(n, carry):
        lo = pl.multiple_of(n * LANES, LANES)
        gate = gates[:, pl.ds(lo, LANES)]
        upper = gates[:, pl.ds(lo + F2, LANES)]
        qh[:, pl.ds(lo + F1, LANES)] = (gate * jax.nn.sigmoid(gate) * upper).astype(BF)
        return carry

    lax.fori_loop(0, F2 // LANES, hidden_once, 0)
    contract_back(qh[:, F1:], F2, w2)
    send_back(0)

    pass_on(1, 0)
    pass_on(1, 1)
    pass_back(0, 0)
    pass_back(0, 1)
    take(1, 0, mat_c)
    take(1, 1, mat_c)

    def q_once(n, carry):
        lo = pl.multiple_of(n * LANES, LANES)
        grad = jnp.dot(mat_c[...], w2[:, pl.ds(lo, LANES)], preferred_element_type=F32)
        gate = gates[:, pl.ds(lo, LANES)]
        upper = gates[:, pl.ds(lo + F2, LANES)]
        sig = jax.nn.sigmoid(gate)
        qh[:, pl.ds(lo, LANES)] = (grad * upper * sig * (1.0 + gate * (1.0 - sig))).astype(BF)
        qh[:, pl.ds(lo + F2, LANES)] = (grad * (gate * sig)).astype(BF)
        return carry

    lax.fori_loop(0, F2 // LANES, q_once, 0)

    def turn_once(n, carry):
        lo = pl.multiple_of(n * LANES, LANES)
        same = lax.broadcasted_iota(jnp.int32, (LANES, LANES), 0) == lax.broadcasted_iota(
            jnp.int32, (LANES, LANES), 1
        )
        one = jnp.where(same, 1.0, 0.0).astype(BF)
        qht[pl.ds(lo, LANES), :] = lax.dot_general(
            one, qh[:, pl.ds(lo, LANES)], NT, preferred_element_type=F32
        ).astype(BF)
        return carry

    lax.fori_loop(0, FF // LANES, turn_once, 0)

    def owner(n):
        ahead = jnp.where(n == 0, 2, jnp.where(n == 1, 1, jnp.where(n == 2, 3, 0)))
        return (x + ahead) % 4

    def twin_copy(n, pair):
        at = owner(n)
        return remote(
            part.at[at, pl.ds(pair * 2, 2), pl.ds((1 - c) * FHALF, FHALF)],
            other.at[at, pl.ds(pair * 2, 2)],
            cs.at[n, pair],
            cr.at[n, pair],
            twin,
        )

    def part_once(i, carry):
        n, pair = i // 2, i % 2
        at = owner(n)

        def columns(mat):
            first = pl.multiple_of((pair * 8 + at) * LANES, LANES)
            second = pl.multiple_of((pair * 8 + 4 + at) * LANES, LANES)
            return jnp.concatenate([mat[:, pl.ds(first, LANES)], mat[:, pl.ds(second, LANES)]], axis=1)

        for lo, right in ((0, mat_x), (F2, mat_x), (F1, mat_c)):
            out = jnp.dot(qht[lo : lo + F2, :], columns(right), preferred_element_type=F32).astype(BF)
            part[at, pair * 2, lo : lo + F2] = out[:, :LANES]
            part[at, pair * 2 + 1, lo : lo + F2] = out[:, LANES:]
        twin_copy(n, pair).start()
        return carry

    lax.fori_loop(0, 8, part_once, 0)

    contract_back(qh[:, :F1], F1, w1)
    send_back(1)

    def relay_copy(q, way):
        return remote(
            summed.at[(x + 2) % 4, :, pl.ds(q * FQ + way * FD, FD)],
            xrelay.at[q, way],
            xs.at[q, way],
            xr.at[q, way],
            x_dev(1 - 2 * way),
        )

    def right_copy(q, way):
        src = xacc.at[q, 0] if way == 0 else summed.at[(x + 1) % 4, :, pl.ds(q * FQ + FD, FD)]
        return remote(src, from_l.at[q, :, pl.ds(way * FD, FD)], xs.at[q, 2 + way], xr.at[q, 2 + way], x_dev(1))

    def left_copy(q, way):
        src = xacc.at[q, 1] if way == 1 else summed.at[(x + 3) % 4, :, pl.ds(q * FQ, FD)]
        return remote(src, from_r.at[q, :, pl.ds(way * FD, FD)], xs.at[q, 4 + way], xr.at[q, 4 + way], x_dev(-1))

    def add_twin(n):
        for pair in range(2):
            twin_copy(n, pair).wait_recv()
        at = owner(n)

        def once(k, carry):
            summed[at, k] = part[at, k, pl.ds(pl.multiple_of(c * FHALF, FHALF), FHALF)] + other[at, k]
            return carry

        lax.fori_loop(0, 4, once, 0)

    add_twin(0)
    for q in range(2):
        for way in range(2):
            relay_copy(q, way).start()
    add_twin(1)
    for q in range(2):
        right_copy(q, 1).start()
    add_twin(2)
    for q in range(2):
        left_copy(q, 0).start()
    add_twin(3)
    for q in range(2):
        for way, ahead in ((0, 1), (1, 3)):
            relay_copy(q, way).wait_recv()
            xacc[q, way] = summed[(x + ahead) % 4, :, q * FQ + way * FD : q * FQ + way * FD + FD] + xrelay[q, way]
            (right_copy if way == 0 else left_copy)(q, way).start()

    pass_back(1, 0)
    pass_back(1, 1)

    def zrelay_copy(q, way):
        return remote(
            zsum.at[q, (zh + 2) % 4, pl.ds(way * FD, FD)], zrelay.at[q, way], gs.at[q, way], gr.at[q, way],
            z_dev(4 - 8 * way),
        )

    def up_copy(q, way):
        src = zacc.at[q, 0] if way == 0 else zsum.at[q, (zh + 1) % 4, pl.ds(FD, FD)]
        return remote(src, zfrom_l.at[q, pl.ds(way * FD, FD)], gs.at[q, 2 + way], gr.at[q, 2 + way], z_dev(4))

    def down_copy(q, way):
        src = zacc.at[q, 1] if way == 1 else zsum.at[q, (zh + 3) % 4, pl.ds(0, FD)]
        return remote(src, zfrom_r.at[q, pl.ds(way * FD, FD)], gs.at[q, 4 + way], gr.at[q, 4 + way], z_dev(-4))

    for q in range(2):
        for way in range(2):
            right_copy(q, 1 - way).wait_recv()
            left_copy(q, way).wait_recv()

        def once(k, carry):
            zsum[q, k] = (
                summed[x, k, q * FQ : (q + 1) * FQ].astype(F32)
                + from_l[q, k].astype(F32)
                + from_r[q, k].astype(F32)
            ).astype(BF)
            return carry

        lax.fori_loop(0, 4, once, 0)
        for way in range(2):
            zrelay_copy(q, way).start()
        up_copy(q, 1).start()
        down_copy(q, 0).start()

    def combine(a, scale, out_ref):
        for h in range(2):
            over_steps(lambda step: ry_copy(a, h, step).wait_recv())
            ry_self(a, h).wait()
        back = backs[a]

        def once(i, carry):
            base = i * 32
            first = jnp.stack([back[group[base + t], inner[base + t]] for t in range(16)])
            second = jnp.stack([back[group[base + 16 + t], inner[base + 16 + t]] for t in range(16)])
            out = from_tiles(first, second)
            lo = pl.multiple_of(base, 32)
            for k in range(16):
                cols = slice(k * LANES, (k + 1) * LANES)
                for half in range(2):
                    rows = pl.ds(lo + half * 16, 16)
                    piece = out[k * 16 : (k + 1) * 16, half * LANES : (half + 1) * LANES]
                    if scale:
                        piece = weight[rows, :] * piece
                    out_ref[rows, cols] = piece.astype(BF)
            return carry

        lax.fori_loop(0, 4, once, 0)

    combine(0, True, mixed)

    for q in range(2):
        for way, ahead in ((0, 1), (1, 3)):
            zrelay_copy(q, way).wait_recv()
            zacc[q, way] = zsum[q, (zh + ahead) % 4, way * FD : way * FD + FD] + zrelay[q, way]
            (up_copy if way == 0 else down_copy)(q, way).start()

    def share_copy(q):
        rows = pl.ds(c * FHALF + q * FQ, FQ)
        return remote(final.at[rows], final.at[rows], fs.at[q], fr.at[q], twin)

    for q in range(2):
        for way in range(2):
            up_copy(q, 1 - way).wait_recv()
            down_copy(q, way).wait_recv()
        total = zsum[q, zh].astype(F32) + zfrom_l[q].astype(F32) + zfrom_r[q].astype(F32)
        final[pl.ds(pl.multiple_of(c * FHALF + q * FQ, FQ), FQ)] = (total * (1.0 / 32.0)).astype(BF)
        share_copy(q).start()

    combine(1, False, token_grad)

    for q in range(2):
        share_copy(q).wait_recv()
    pick = (
        lax.broadcasted_iota(jnp.int32, (64, LANES), 1) == lax.broadcasted_iota(jnp.int32, (64, LANES), 0) + c * 64
    )
    pick = jnp.where(pick, 1.0, 0.0).astype(BF)
    grad_in[0] = lax.dot_general(pick, final[:F1], NT, preferred_element_type=F32).astype(BF)
    grad_out[0] = lax.dot_general(pick, final[F1:], NT, preferred_element_type=F32).astype(BF)

    for a in range(2):
        for h in range(2):
            over_steps(lambda step: y_copy(a, h, step).wait_send())
            over_steps(lambda step: ry_copy(a, h, step).wait_send())
            for k in (0, 2, 3):
                z_copy(a, h, k).wait_send()
                rz_copy(a, h, k).wait_send()
    for n in range(4):
        for pair in range(2):
            twin_copy(n, pair).wait_send()
    for q in range(2):
        for way in range(2):
            relay_copy(q, way).wait_send()
            right_copy(q, way).wait_send()
            left_copy(q, way).wait_send()
            zrelay_copy(q, way).wait_send()
            up_copy(q, way).wait_send()
            down_copy(q, way).wait_send()
        share_copy(q).wait_send()


def per_device(tokens, routes, route_weight, w_in, w_out, out_grad):
    source, group, inner = slot_tables(routes)
    smem = pl.BlockSpec(memory_space=pltpu.SMEM)
    vmem = pl.BlockSpec(memory_space=pltpu.VMEM)
    anywhere = pl.BlockSpec(memory_space=pl.ANY)
    dma = pltpu.SemaphoreType.DMA
    tile = (TILE, LANES)
    return pl.pallas_call(
        kernel,
        name="moe",
        out_shape=(
            jax.ShapeDtypeStruct((TOK, D), BF),
            jax.ShapeDtypeStruct((TOK, D), BF),
            jax.ShapeDtypeStruct((1, 64, F1), BF),
            jax.ShapeDtypeStruct((1, 64, F2), BF),
        ),
        in_specs=[smem, smem, smem, vmem, vmem, vmem, anywhere, anywhere],
        out_specs=(vmem, vmem, vmem, vmem),
        scratch_shapes=[
            pltpu.VMEM((D, F1), BF),
            pltpu.VMEM((D, F2), BF),
            pltpu.VMEM((256, 256), BF),
            pltpu.VMEM((TOK + 1, *tile), BF),
            pltpu.VMEM((TOK + 1, *tile), BF),
            pltpu.VMEM((2, 2, 32, 3, *tile), BF),
            pltpu.VMEM((2, 2, 4, 24, *tile), BF),
            pltpu.VMEM((2, 2, 96, *tile), BF),
            pltpu.VMEM((ROWS, D), BF),
            pltpu.VMEM((ROWS, D), BF),
            pltpu.VMEM((ROWS, F1), F32),
            pltpu.VMEM((ROWS, FF), BF),
            pltpu.VMEM((FF, ROWS), BF),
            pltpu.VMEM((ROWS, D), BF),
            pltpu.VMEM((2, 2, 96, *tile), BF),
            pltpu.VMEM((2, 2, 4, 24, *tile), BF),
            pltpu.VMEM((64, 3, *tile), BF),
            pltpu.VMEM((64, 3, *tile), BF),
            pltpu.VMEM((4, 4, FF, LANES), BF),
            pltpu.VMEM((4, 4, FHALF, LANES), BF),
            pltpu.VMEM((4, 4, FHALF, LANES), BF),
            pltpu.VMEM((2, 2, 4, FD, LANES), BF),
            pltpu.VMEM((2, 2, 4, FD, LANES), BF),
            pltpu.VMEM((2, 4, FQ, LANES), BF),
            pltpu.VMEM((2, 4, FQ, LANES), BF),
            pltpu.VMEM((2, 4, FQ, LANES), BF),
            pltpu.VMEM((2, 2, FD, LANES), BF),
            pltpu.VMEM((2, 2, FD, LANES), BF),
            pltpu.VMEM((2, FQ, LANES), BF),
            pltpu.VMEM((2, FQ, LANES), BF),
            pltpu.VMEM((FF, LANES), BF),
            dma((2,)),
            dma((2, 2, 7)), dma((2, 2, 7)), dma((2, 2)),
            dma((2, 2, 4)), dma((2, 2, 4)), dma((2, 2)),
            dma((2, 2, 4)), dma((2, 2, 4)), dma((2, 2)),
            dma((2, 2, 7)), dma((2, 2, 7)), dma((2, 2)),
            dma((4, 2)), dma((4, 2)),
            dma((2, 6)), dma((2, 6)),
            dma((2, 6)), dma((2, 6)),
            dma((2,)), dma((2,)),
        ],
        compiler_params=pltpu.CompilerParams(
            collective_id=0, has_side_effects=True, vmem_limit_bytes=52 << 20
        ),
    )(source, group, inner, tokens, out_grad, route_weight, w_in, w_out)


def solution(mesh):
    rows = P(("expert", "dp"), None)
    whole = P("expert", None, None)
    return jax.shard_map(
        per_device,
        mesh=mesh,
        in_specs=(rows, rows, rows, whole, whole, rows),
        out_specs=(rows, rows, P("expert", "dp", None), P("expert", "dp", None)),
        check_vma=False,
    )
```

time: 376 us -> 131 us (0.35)
  the two profiles are of different devices: /device:TPU:16 before, /device:TPU:25 now
where the time goes in v1:
time: 131 us
  Pallas kernels  124 us (95%)
  local copies, waits for them, and re-layouts  4.65 us (4%)
  other arithmetic  1.7 us (1%)
    pallas_call x1, Pallas kernels, per_device(): pl.pallas_call(kernel, name='moe', out_shape=(jax.ShapeDtypeStruct((TOK,...  124 us
    unnamed x7, local copies, waits for them, and re-layouts  4.65 us

profile of v1, /device:TPU:25, one launch (start us, length us, event | category | flops | bytes accessed | tf_op | source)
XLA Modules:
  0.0 130.9 jit_solution(4184009715236664888)
XLA Ops:
  0.6 0.9 convert_reduce_fusion
  1.5 0.7 multiply_add_fusion
  2.2 0.1 select_reduce_fusion
  2.3 0.8 copy.11.weight
  3.1 0.0 copy-start
  3.1 1.0 copy-done
  4.1 123.9 %moe.1 = (bf16[128,2048]{1,0:T(8,128)(2,1)S(1)}, bf16[128,2048]{1,0:T(8,128)(2,1)S(1)}, bf16[1,64,768]{2,1,0:T(8,128)(2,1)S(1)}, bf16[1,64,384]{2,1,0:T(8,128)(2,1)S(1)}) custom-call(s32[192]{0:T(256)S(1)} %broadcast_add_fusion.source, s32[128]{0:T(128)S(1)} %get-tuple-element.5.group, s32[128]{0:T(128)S(1)} %get-tuple-element.6.inner, ...), custom_call_target="tpu_custom_call" | custom-call | tf_op jit(solution)/shard_map/moe/pallas_call | solution.py:529
  128.1 0.8 copy.16
  128.9 0.8 copy.17
  129.7 0.6 copy.18
  130.3 0.6 copy.19
  (1 shorter events, 0.0 us)
Async XLA Ops:
  3.1 1.0 copy-start

commit v2 on v1

v2 whole, which is shorter than its diff:
```python
import functools

import jax
import jax.numpy as jnp
from jax import lax
from jax.experimental import pallas as pl
from jax.experimental.pallas import tpu as pltpu
from jax.sharding import PartitionSpec as P

MESH = pl.DeviceIdType.MESH
BF = jnp.bfloat16
F32 = jnp.float32

D = 2048
F1 = 768
F2 = 384
FF = F1 + F2
ROWS = 192
TOK = 128
LANES = 128
TILE = 16
NH = 3
SP = 6 // NH
PART = ROWS // NH
FHALF = FF // 2
NQ = 6
FQ = FHALF // NQ
FD = FQ // 2
NT = (((1,), (1,)), ((), ()))
WINDOW = (-1, 0, 1, 2)


def kernel(
    routes, weights, tokens_any, grad_any, w1_any, w2_any,
    mixed, token_grad, grad_in, grad_out,
    tokens, out_grad, weight, table, slots, w1, w2, perm, tiles_t, tiles_c, stage, mid, landed, mat_x, mat_c, gates, qh, qht, mat_y,
    ytile, zback, back_y, back_r, part, other, summed,
    xrelay, xacc, from_l, from_r, zsum, zrelay, zacc, zfrom_l, zfrom_r, final,
    io_sem, w_sem, ys, yr, yl, zs, zr, zl_sem, rzs, rzr, rzl, rys, ryr, ryl,
    cs, cr, xs, xr, gs, gr, fs, fr,
):
    e = lax.axis_index("expert")
    d = lax.axis_index("dp")
    y, zl = e // 4, e % 4
    zh, x, c = d // 8, (d // 2) % 4, d % 2
    z = zh * 4 + zl
    sign = 1 - 2 * c

    def device(y_at, z_at, x_at, c_at):
        return {"expert": y_at * 4 + z_at % 4, "dp": (z_at // 4) * 8 + x_at * 2 + c_at}

    def y_dev(step):
        return device((y + step) % 8, z, x, c)

    def z_dev(step):
        return device(y, (z + step + 16) % 16, x, c)

    def x_dev(step):
        return device(y, z, (x + step + 4) % 4, c)

    twin = device(y, z, x, 1 - c)

    def remote(src, dst, send, recv, to):
        return pltpu.make_async_remote_copy(
            src_ref=src, dst_ref=dst, send_sem=send, recv_sem=recv, device_id=to, device_id_type=MESH
        )

    io_copies = (
        pltpu.make_async_copy(tokens_any, tokens, io_sem.at[0]),
        pltpu.make_async_copy(grad_any, out_grad, io_sem.at[1]),
    )
    w_copies = (
        pltpu.make_async_copy(w1_any.at[0], w1, w_sem.at[0]),
        pltpu.make_async_copy(w2_any.at[0], w2, w_sem.at[1]),
    )
    for copy in io_copies:
        copy.start()
    barrier = pltpu.get_barrier_semaphore()

    def greet(to):
        pl.semaphore_signal(barrier, inc=1, device_id=to, device_id_type=MESH)

    for step in range(1, 8):
        greet(y_dev(step))
    for step in (-4, -2, -1, 1, 2, 4):
        greet(z_dev(step))
    for step in (-1, 1):
        greet(x_dev(step))
    greet(twin)

    for copy in w_copies:
        copy.start()

    chosen = routes[...]
    by_col = jnp.broadcast_to(chosen.astype(F32), (TOK, TOK))
    earlier = lax.broadcasted_iota(jnp.int32, (TOK, TOK), 0) < lax.broadcasted_iota(jnp.int32, (TOK, TOK), 1)
    same = (by_col == jnp.transpose(by_col)) & earlier
    rank = jnp.sum(jnp.where(same, 1, 0), axis=0, keepdims=True)
    group_of = (rank // SP) * 32 + chosen
    inner_of = rank % SP
    place = jnp.broadcast_to((group_of * SP + inner_of).astype(F32), (2 * TOK, TOK))
    slot_at = lax.broadcasted_iota(jnp.int32, (TOK, 2 * TOK), 1).astype(F32)
    token_at = lax.broadcasted_iota(jnp.int32, (TOK, 2 * TOK), 0)
    holds = jnp.transpose(place) == slot_at
    table[...] = jnp.zeros_like(table)
    token_of = TOK + jnp.sum(jnp.where(holds, token_at - TOK, 0), axis=0, keepdims=True)
    table[0:1, :] = jnp.clip(token_of, 0, TOK)
    table[1:2, :TOK] = jnp.clip(group_of, 0, NH * 32 - 1)
    table[2:3, :TOK] = inner_of
    table_copy = pltpu.make_async_copy(table, slots, io_sem.at[2])
    table_copy.start()
    weight[...] = jnp.transpose(jnp.broadcast_to(weights[...], (TOK, TOK)))

    row_at = lax.broadcasted_iota(jnp.int32, (256, 256), 0)
    col_at = lax.broadcasted_iota(jnp.int32, (256, 256), 1)
    perm[...] = jnp.where(col_at == (row_at % 16) * 16 + row_at // 16, 1.0, 0.0).astype(BF)

    def to_tiles(rows32):
        cols = [
            jnp.concatenate(
                [rows32[:16, k * LANES : (k + 1) * LANES], rows32[16:, k * LANES : (k + 1) * LANES]], axis=1
            )
            for k in range(16)
        ]
        out = jnp.dot(perm[...], jnp.concatenate(cols, axis=0), preferred_element_type=F32).astype(BF)
        return out[:, :LANES].reshape(16, TILE, LANES), out[:, LANES:].reshape(16, TILE, LANES)

    def from_tiles(first, second):
        both = jnp.concatenate([first.reshape(256, LANES), second.reshape(256, LANES)], axis=1)
        return jnp.dot(perm[...], both, preferred_element_type=F32)

    tiles_t[TOK] = jnp.zeros((TILE, LANES), BF)
    tiles_c[TOK] = jnp.zeros((TILE, LANES), BF)

    def y_copy(a, h, step):
        there = (y + step) % 8
        return remote(
            stage.at[a, h, pl.ds(there * 4, 4)],
            mid.at[a, h, :, pl.ds(y * SP, SP)],
            ys.at[a, h, step - 1],
            yr.at[a, h, step - 1],
            y_dev(step),
        )

    def y_self(a, h):
        return pltpu.make_async_copy(
            stage.at[a, h, pl.ds(y * 4, 4)], mid.at[a, h, :, pl.ds(y * SP, SP)], yl.at[a, h]
        )

    def step_of(n):
        half = n // 2 + 1
        return half + (n % 2) * (8 - 2 * half)

    def over_steps(body):
        def once(n, carry):
            body(step_of(n))
            return carry

        lax.fori_loop(0, 7, once, 0)

    def split_tokens(i, carry):
        lo, hi = to_tiles(tokens[pl.ds(i * 32, 32), :])
        tiles_t[pl.ds(i * 32, 16)] = lo
        tiles_t[pl.ds(i * 32 + 16, 16)] = hi
        return carry

    io_copies[0].wait()
    lax.fori_loop(0, 4, split_tokens, 0, unroll=2)

    def gather(a, h, tiles):
        def once(i, carry):
            for s in range(SP):
                stage[a, h, i, s] = tiles[slots[0, (h * 32 + i) * SP + s]]
            return carry

        lax.fori_loop(0, 32, once, 0, unroll=4)

    def y_start(a, h):
        over_steps(lambda step: y_copy(a, h, step).start())
        y_self(a, h).start()

    table_copy.wait()
    gather(0, 0, tiles_t)
    pl.semaphore_wait(barrier, 16)
    y_start(0, 0)
    for h in range(1, NH):
        gather(0, h, tiles_t)
        y_start(0, h)

    def split_cot(i, carry):
        rows = pl.ds(i * 32, 32)
        scale = jnp.concatenate([weight[rows, :]] * 16, axis=1)
        cot = (scale * out_grad[rows, :].astype(F32)).astype(BF)
        lo, hi = to_tiles(cot)
        tiles_c[pl.ds(i * 32, 16)] = lo
        tiles_c[pl.ds(i * 32 + 16, 16)] = hi
        return carry

    io_copies[1].wait()
    lax.fori_loop(0, 4, split_cot, 0, unroll=2)
    for h in range(NH):
        gather(1, h, tiles_c)

    def z_copy(a, h, k):
        to = (z + sign * WINDOW[k] + 16) % 16
        return remote(
            mid.at[a, h, to % 4], landed.at[a, h, pl.ds(k * 8 * SP, 8 * SP)], zs.at[a, h, k], zr.at[a, h, k],
            device(y, to, x, c),
        )

    def z_self(a, h):
        return pltpu.make_async_copy(mid.at[a, h, zl], landed.at[a, h, pl.ds(8 * SP, 8 * SP)], zl_sem.at[a, h])

    def pass_on(a, h):
        over_steps(lambda step: y_copy(a, h, step).wait_recv())
        y_self(a, h).wait()
        for k in (3, 0, 2):
            z_copy(a, h, k).start()
        z_self(a, h).start()

    def take(a, h, mat):
        for k in (0, 2, 3):
            z_copy(a, h, k).wait_recv()
        z_self(a, h).wait()

        def once(i, carry):
            out = from_tiles(landed[a, h, pl.ds(i * 32, 16)], landed[a, h, pl.ds(i * 32 + 16, 16)])
            lo = pl.multiple_of(h * PART + i * 32, 32)
            for k in range(16):
                cols = slice(k * LANES, (k + 1) * LANES)
                mat[pl.ds(lo, 16), cols] = out[k * 16 : (k + 1) * 16, :LANES].astype(BF)
                mat[pl.ds(lo + 16, 16), cols] = out[k * 16 : (k + 1) * 16, LANES:].astype(BF)
            return carry

        lax.fori_loop(0, PART // 32, once, 0, unroll=True)

    def rz_copy(a, h, k):
        to = (z - sign * WINDOW[k] + 16) % 16
        return remote(
            ytile.at[a, h, pl.ds(k * 8 * SP, 8 * SP)], zback.at[a, h, zl], rzs.at[a, h, k], rzr.at[a, h, k],
            device(y, to, x, c),
        )

    def rz_self(a, h):
        return pltpu.make_async_copy(ytile.at[a, h, pl.ds(8 * SP, 8 * SP)], zback.at[a, h, zl], rzl.at[a, h])

    backs = (back_y, back_r)

    def ry_copy(a, h, step):
        there = (y + step) % 8
        return remote(
            zback.at[a, h, :, pl.ds(there * SP, SP)],
            backs[a].at[pl.ds(h * 32 + y * 4, 4)],
            rys.at[a, h, step - 1],
            ryr.at[a, h, step - 1],
            y_dev(step),
        )

    def ry_self(a, h):
        return pltpu.make_async_copy(
            zback.at[a, h, :, pl.ds(y * SP, SP)], backs[a].at[pl.ds(h * 32 + y * 4, 4)], ryl.at[a, h]
        )

    def z_back(a, h):
        for k in (3, 0, 2):
            rz_copy(a, h, k).start()
        rz_self(a, h).start()

    def send_back(a, now):
        for h in range(NH):
            def once(i, carry):
                lo, hi = to_tiles(mat_y[pl.ds(pl.multiple_of(h * PART + i * 32, 32), 32), :])
                ytile[a, h, pl.ds(i * 32, 16)] = lo
                ytile[a, h, pl.ds(i * 32 + 16, 16)] = hi
                return carry

            lax.fori_loop(0, PART // 32, once, 0, unroll=True)
            if h < now:
                z_back(a, h)

    def pass_back(a, h):
        for k in (0, 2, 3):
            rz_copy(a, h, k).wait_recv()
        rz_self(a, h).wait()
        over_steps(lambda step: ry_copy(a, h, step).start())
        ry_self(a, h).start()

    def contract_back(left, width, weights):
        def once(n, carry):
            at = pl.multiple_of(n * 256, 256)
            out = lax.dot_general(left, weights[pl.ds(at, 256), :], NT, preferred_element_type=F32)
            mat_y[:, pl.ds(at, 256)] = out.astype(BF)
            return carry

        lax.fori_loop(0, D // 256, once, 0, unroll=2)

    for copy in w_copies:
        copy.wait()
    for h in range(NH):
        pass_on(0, h)
        y_start(1, h)
    for h in range(NH):
        take(0, h, mat_x)

    def gates_once(n, carry):
        at = pl.multiple_of(n * 256, 256)
        gates[:, pl.ds(at, 256)] = jnp.dot(mat_x[...], w1[:, pl.ds(at, 256)], preferred_element_type=F32)
        return carry

    lax.fori_loop(0, F1 // 256, gates_once, 0, unroll=True)

    def hidden_once(n, carry):
        lo = pl.multiple_of(n * LANES, LANES)
        gate = gates[:, pl.ds(lo, LANES)]
        upper = gates[:, pl.ds(lo + F2, LANES)]
        qh[:, pl.ds(lo + F1, LANES)] = (gate * jax.nn.sigmoid(gate) * upper).astype(BF)
        return carry

    lax.fori_loop(0, F2 // LANES, hidden_once, 0, unroll=True)
    pass_on(1, 0)
    contract_back(qh[:, F1:], F2, w2)
    send_back(0, 1)

    for h in range(1, NH):
        pass_on(1, h)
    pass_back(0, 0)
    for h in range(NH):
        take(1, h, mat_c)
        if h >= 1:
            z_back(0, h)

    def q_once(n, carry):
        lo = pl.multiple_of(n * LANES, LANES)
        grad = jnp.dot(mat_c[...], w2[:, pl.ds(lo, LANES)], preferred_element_type=F32)
        gate = gates[:, pl.ds(lo, LANES)]
        upper = gates[:, pl.ds(lo + F2, LANES)]
        sig = jax.nn.sigmoid(gate)
        qh[:, pl.ds(lo, LANES)] = (grad * upper * sig * (1.0 + gate * (1.0 - sig))).astype(BF)
        qh[:, pl.ds(lo + F2, LANES)] = (grad * (gate * sig)).astype(BF)
        return carry

    lax.fori_loop(0, F2 // LANES, q_once, 0, unroll=True)

    def turn_once(n, carry):
        lo = pl.multiple_of(n * LANES, LANES)
        same = lax.broadcasted_iota(jnp.int32, (LANES, LANES), 0) == lax.broadcasted_iota(
            jnp.int32, (LANES, LANES), 1
        )
        one = jnp.where(same, 1.0, 0.0).astype(BF)
        qht[pl.ds(lo, LANES), :] = lax.dot_general(
            one, qh[:, pl.ds(lo, LANES)], NT, preferred_element_type=F32
        ).astype(BF)
        return carry

    lax.fori_loop(0, FF // LANES, turn_once, 0, unroll=3)

    def owner(n):
        return (x + (2, 1, 3, 0)[n]) % 4

    def twin_copy(n, pair):
        at = owner(n)
        return remote(
            part.at[at, pl.ds(pair * 2, 2), pl.ds((1 - c) * FHALF, FHALF)],
            other.at[at, pl.ds(pair * 2, 2)],
            cs.at[n, pair],
            cr.at[n, pair],
            twin,
        )

    def part_once(n, pair):
        at = owner(n)

        def columns(mat):
            first = pl.multiple_of((pair * 8 + at) * LANES, LANES)
            second = pl.multiple_of((pair * 8 + 4 + at) * LANES, LANES)
            return jnp.concatenate([mat[:, pl.ds(first, LANES)], mat[:, pl.ds(second, LANES)]], axis=1)

        for lo, right in ((0, mat_x), (F2, mat_x), (F1, mat_c)):
            out = jnp.dot(qht[lo : lo + F2, :], columns(right), preferred_element_type=F32).astype(BF)
            part[at, pair * 2, lo : lo + F2] = out[:, :LANES]
            part[at, pair * 2 + 1, lo : lo + F2] = out[:, LANES:]
        twin_copy(n, pair).start()

    def relay_copy(q, way):
        return remote(
            summed.at[(x + 2) % 4, :, pl.ds(q * FQ + way * FD, FD)],
            xrelay.at[q, way],
            xs.at[q, way],
            xr.at[q, way],
            x_dev(1 - 2 * way),
        )

    def right_copy(q, way):
        src = xacc.at[q, 0] if way == 0 else summed.at[(x + 1) % 4, :, pl.ds(q * FQ + FD, FD)]
        return remote(src, from_l.at[q, :, pl.ds(way * FD, FD)], xs.at[q, 2 + way], xr.at[q, 2 + way], x_dev(1))

    def left_copy(q, way):
        src = xacc.at[q, 1] if way == 1 else summed.at[(x + 3) % 4, :, pl.ds(q * FQ, FD)]
        return remote(src, from_r.at[q, :, pl.ds(way * FD, FD)], xs.at[q, 4 + way], xr.at[q, 4 + way], x_dev(-1))

    def add_twin(n):
        for pair in range(2):
            twin_copy(n, pair).wait_recv()
        at = owner(n)

        def once(k, carry):
            summed[at, k] = part[at, k, pl.ds(pl.multiple_of(c * FHALF, FHALF), FHALF)] + other[at, k]
            return carry

        lax.fori_loop(0, 4, once, 0)

    def zrelay_copy(q, way):
        return remote(
            zsum.at[q, (zh + 2) % 4, pl.ds(way * FD, FD)], zrelay.at[q, way], gs.at[q, way], gr.at[q, way],
            z_dev(4 - 8 * way),
        )

    def up_copy(q, way):
        src = zacc.at[q, 0] if way == 0 else zsum.at[q, (zh + 1) % 4, pl.ds(FD, FD)]
        return remote(src, zfrom_l.at[q, pl.ds(way * FD, FD)], gs.at[q, 2 + way], gr.at[q, 2 + way], z_dev(4))

    def down_copy(q, way):
        src = zacc.at[q, 1] if way == 1 else zsum.at[q, (zh + 3) % 4, pl.ds(0, FD)]
        return remote(src, zfrom_r.at[q, pl.ds(way * FD, FD)], gs.at[q, 4 + way], gr.at[q, 4 + way], z_dev(-4))

    def combine(a, scale, out_ref):
        for h in range(NH):
            over_steps(lambda step: ry_copy(a, h, step).wait_recv())
            ry_self(a, h).wait()
        back = backs[a]

        def once(i, carry):
            base = i * 32
            first = jnp.stack([back[slots[1, base + t], slots[2, base + t]] for t in range(16)])
            second = jnp.stack([back[slots[1, base + 16 + t], slots[2, base + 16 + t]] for t in range(16)])
            out = from_tiles(first, second)
            lo = pl.multiple_of(base, 32)
            for k in range(16):
                cols = slice(k * LANES, (k + 1) * LANES)
                for half in range(2):
                    rows = pl.ds(lo + half * 16, 16)
                    piece = out[k * 16 : (k + 1) * 16, half * LANES : (half + 1) * LANES]
                    if scale:
                        piece = weight[rows, :] * piece
                    out_ref[rows, cols] = piece.astype(BF)
            return carry

        lax.fori_loop(0, 4, once, 0)

    def share_copy(q):
        rows = pl.ds(c * FHALF + q * FQ, FQ)
        return remote(final.at[rows], final.at[rows], fs.at[q], fr.at[q], twin)

    def x_relay(q):
        for way in range(2):
            relay_copy(q, way).start()

    def x_start(q):
        right_copy(q, 1).start()
        left_copy(q, 0).start()

    def x_forward(q):
        for way, ahead in ((0, 1), (1, 3)):
            relay_copy(q, way).wait_recv()
            lo = q * FQ + way * FD
            xacc[q, way] = summed[(x + ahead) % 4, :, lo : lo + FD] + xrelay[q, way]
            (right_copy if way == 0 else left_copy)(q, way).start()

    def z_start(q):
        for way in range(2):
            right_copy(q, 1 - way).wait_recv()
            left_copy(q, way).wait_recv()
        zsum[q] = (
            summed[x, :, q * FQ : (q + 1) * FQ].astype(F32) + from_l[q].astype(F32) + from_r[q].astype(F32)
        ).astype(BF)
        for way in range(2):
            zrelay_copy(q, way).start()
        up_copy(q, 1).start()
        down_copy(q, 0).start()

    def z_forward(q):
        for way, ahead in ((0, 1), (1, 3)):
            zrelay_copy(q, way).wait_recv()
            zacc[q, way] = zsum[q, (zh + ahead) % 4, way * FD : way * FD + FD] + zrelay[q, way]
            (up_copy if way == 0 else down_copy)(q, way).start()

    def share_start(q):
        for way in range(2):
            up_copy(q, 1 - way).wait_recv()
            down_copy(q, way).wait_recv()
        total = zsum[q, zh].astype(F32) + zfrom_l[q].astype(F32) + zfrom_r[q].astype(F32)
        final[pl.ds(pl.multiple_of(c * FHALF + q * FQ, 32), FQ)] = (total * (1.0 / 32.0)).astype(BF)
        share_copy(q).start()

    for n in range(4):
        for pair in range(2):
            part_once(n, pair)
    pass_back(0, 1)
    add_twin(0)
    for q in range(3):
        x_relay(q)
    add_twin(1)
    for q in range(2):
        right_copy(q, 1).start()
    add_twin(2)
    for q in range(2):
        left_copy(q, 0).start()
    add_twin(3)
    contract_back(qh[:, :F1], F1, w1)
    send_back(1, NH)
    pass_back(0, 2)

    for s in range(NQ + 8):
        if s < NQ:
            x_forward(s)
        if s + 3 < NQ:
            x_relay(s + 3)
        if s + 2 < NQ:
            x_start(s + 2)
        if 2 <= s <= NQ + 1:
            z_start(s - 2)
        if 2 <= s < NH + 2:
            pass_back(1, s - 2)
        if 5 <= s <= NQ + 4:
            z_forward(s - 5)
        if 8 <= s:
            share_start(s - 8)
        if s == NQ + 2:
            combine(0, True, mixed)

    combine(1, False, token_grad)

    for q in range(NQ):
        share_copy(q).wait_recv()
    pick = (
        lax.broadcasted_iota(jnp.int32, (64, LANES), 1) == lax.broadcasted_iota(jnp.int32, (64, LANES), 0) + c * 64
    )
    pick = jnp.where(pick, 1.0, 0.0).astype(BF)
    grad_in[0] = lax.dot_general(pick, final[:F1], NT, preferred_element_type=F32).astype(BF)
    grad_out[0] = lax.dot_general(pick, final[F1:], NT, preferred_element_type=F32).astype(BF)

    for a in range(2):
        for h in range(NH):
            over_steps(lambda step: y_copy(a, h, step).wait_send())
            over_steps(lambda step: ry_copy(a, h, step).wait_send())
            for k in (0, 2, 3):
                z_copy(a, h, k).wait_send()
                rz_copy(a, h, k).wait_send()
    for n in range(4):
        for pair in range(2):
            twin_copy(n, pair).wait_send()
    for q in range(NQ):
        for way in range(2):
            relay_copy(q, way).wait_send()
            right_copy(q, way).wait_send()
            left_copy(q, way).wait_send()
            zrelay_copy(q, way).wait_send()
            up_copy(q, way).wait_send()
            down_copy(q, way).wait_send()
        share_copy(q).wait_send()


def per_device(tokens, routes, route_weight, w_in, w_out, out_grad):
    vmem = pl.BlockSpec(memory_space=pltpu.VMEM)
    anywhere = pl.BlockSpec(memory_space=pltpu.HBM)
    dma = pltpu.SemaphoreType.DMA
    tile = (TILE, LANES)
    shapes = (
        jax.ShapeDtypeStruct((TOK, D), BF),
        jax.ShapeDtypeStruct((TOK, D), BF),
        jax.ShapeDtypeStruct((1, 64, F1), BF),
        jax.ShapeDtypeStruct((1, 64, F2), BF),
    )
    return pl.pallas_call(
        kernel,
        name="moe",
        out_shape=shapes,
        in_specs=[vmem, vmem, anywhere, anywhere, anywhere, anywhere],
        out_specs=(vmem, vmem, vmem, vmem),
        scratch_shapes=[
            pltpu.VMEM((TOK, D), BF),
            pltpu.VMEM((TOK, D), BF),
            pltpu.VMEM((TOK, TOK), F32),
            pltpu.VMEM((8, 2 * TOK), jnp.int32),
            pltpu.SMEM((8, 2 * TOK), jnp.int32),
            pltpu.VMEM((D, F1), BF),
            pltpu.VMEM((D, F2), BF),
            pltpu.VMEM((256, 256), BF),
            pltpu.VMEM((TOK + 1, *tile), BF),
            pltpu.VMEM((TOK + 1, *tile), BF),
            pltpu.VMEM((2, NH, 32, SP, *tile), BF),
            pltpu.VMEM((2, NH, 4, 8 * SP, *tile), BF),
            pltpu.VMEM((2, NH, PART, *tile), BF),
            pltpu.VMEM((ROWS, D), BF),
            pltpu.VMEM((ROWS, D), BF),
            pltpu.VMEM((ROWS, F1), F32),
            pltpu.VMEM((ROWS, FF), BF),
            pltpu.VMEM((FF, ROWS), BF),
            pltpu.VMEM((ROWS, D), BF),
            pltpu.VMEM((2, NH, PART, *tile), BF),
            pltpu.VMEM((2, NH, 4, 8 * SP, *tile), BF),
            pltpu.VMEM((NH * 32, SP, *tile), BF),
            pltpu.VMEM((NH * 32, SP, *tile), BF),
            pltpu.VMEM((4, 4, FF, LANES), BF),
            pltpu.VMEM((4, 4, FHALF, LANES), BF),
            pltpu.VMEM((4, 4, FHALF, LANES), BF),
            pltpu.VMEM((NQ, 2, 4, FD, LANES), BF),
            pltpu.VMEM((NQ, 2, 4, FD, LANES), BF),
            pltpu.VMEM((NQ, 4, FQ, LANES), BF),
            pltpu.VMEM((NQ, 4, FQ, LANES), BF),
            pltpu.VMEM((NQ, 4, FQ, LANES), BF),
            pltpu.VMEM((NQ, 2, FD, LANES), BF),
            pltpu.VMEM((NQ, 2, FD, LANES), BF),
            pltpu.VMEM((NQ, FQ, LANES), BF),
            pltpu.VMEM((NQ, FQ, LANES), BF),
            pltpu.VMEM((FF, LANES), BF),
            dma((3,)),
            dma((2,)),
            dma((2, NH, 7)), dma((2, NH, 7)), dma((2, NH)),
            dma((2, NH, 4)), dma((2, NH, 4)), dma((2, NH)),
            dma((2, NH, 4)), dma((2, NH, 4)), dma((2, NH)),
            dma((2, NH, 7)), dma((2, NH, 7)), dma((2, NH)),
            dma((4, 2)), dma((4, 2)),
            dma((NQ, 6)), dma((NQ, 6)),
            dma((NQ, 6)), dma((NQ, 6)),
            dma((NQ,)), dma((NQ,)),
        ],
        compiler_params=pltpu.CompilerParams(
            collective_id=0, has_side_effects=True, vmem_limit_bytes=52 << 20
        ),
    )(routes.reshape(1, TOK), route_weight.reshape(1, TOK), tokens, out_grad, w_in, w_out)


def solution(mesh):
    rows = P(("expert", "dp"), None)
    whole = P("expert", None, None)
    return jax.shard_map(
        per_device,
        mesh=mesh,
        in_specs=(rows, rows, rows, whole, whole, rows),
        out_specs=(rows, rows, P("expert", "dp", None), P("expert", "dp", None)),
        check_vma=False,
    )
```

time: 131 us -> 122 us (0.931)
  the two profiles are of different devices: /device:TPU:25 before, /device:TPU:14 now
where the time goes in v2:
time: 122 us
  Pallas kernels  116 us (95%)
  local copies, waits for them, and re-layouts  5.19 us (4%)
    pallas_call x1, Pallas kernels, per_device(): pl.pallas_call(kernel, name='moe', out_shape=shapes, in_specs=[vmem, vmem...  116 us
    unnamed x10, local copies, waits for them, and re-layouts  5.19 us

profile of v2, /device:TPU:14, one launch (start us, length us, event | category | flops | bytes accessed | tf_op | source)
XLA Modules:
  0.0 122.1 jit_solution(7470283553788860484)
XLA Ops:
  0.6 0.0 copy-start
  0.6 1.0 copy-done
  1.7 0.0 copy-start.1
  1.7 0.7 copy-done.1
  2.3 0.0 copy-start.2
  2.3 0.7 copy-done.2
  3.0 116.2 %moe.1 = (bf16[128,2048]{1,0:T(8,128)(2,1)S(1)}, bf16[128,2048]{1,0:T(8,128)(2,1)S(1)}, bf16[1,64,768]{2,1,0:T(8,128)(2,1)S(1)}, bf16[1,64,384]{2,1,0:T(8,128)(2,1)S(1)}) custom-call(s32[1,128]{1,0:T(1,128)S(1)} %bitcast.2, f32[1,128]{1,0:T(1,128)S(1)} %bitcast.3, bf16[128,2048]{1,0:T(8,128)(2,1)S(1)} %copy-done, bf16[128,2048]{1,0:T(8,128)(2,1)} %grad_any.1, ...), custom_call_target="tpu_custom_call" | custom-call | tf_op jit(solution)/shard_map/moe/pallas_call | solution.py:574
  119.2 0.8 copy.14
  120.0 0.8 copy.15
  120.8 0.6 copy.16
  121.4 0.6 copy.17
Async XLA Ops:
  0.6 1.0 copy-start
  1.7 0.7 copy-start.1
  2.3 0.7 copy-start.2
